TPU v7x, 32 devices: a whole 2x2x4 slice. The times are simulated.
32 devices in a mesh: groups: 2 (over y), plane: 4 (over z), normal: 2 (over x), inner: 2 (over core).
Axes of the slice: x: 2, y: 2, z: 4, core: 2. Of those that a mesh axis runs over, the one named last changes fastest.
Arguments:
- phase: int32 [64, 64, 256], P(('groups', 'normal'), 'plane', 'inner'), parts along dimension 0, may hold values 0 or 1
- velocity: float32 [3, 64, 64, 256], P(None, ('groups', 'normal'), 'plane', 'inner'), parts along dimension 1, may hold values from -0.75 to 0.75
- stress: float32 [6, 64, 64, 256], P(None, ('groups', 'normal'), 'plane', 'inner'), parts along dimension 1, may hold values from -0.2 to 0.2
- new_slot: int32 [128], P(('groups', 'plane')), parts along dimension 0, may hold values from 0 to 63, as said below
Outputs:
- moved: bfloat16 [10, 64, 64, 256], P(None, ('groups', 'normal'), 'plane', 'inner'), parts along dimension 1
There are 2 independent parts, one for each index of `groups`. A program takes and returns all parts, laid end to end along the dimension named above; each array names one. Nothing has to cross between parts.
Inputs may be any that keep to these rules, and one draw needn't show every extreme that they name: `new_slot`: a permutation of 0 to 63; of the 16 column blocks held by one plane device, at most 4 go to any one plane device, and exactly 4 do in every draw.
All inputs are finite; a program needn't handle non-finite values. No bound on the sum of `phase` on one device may be relied on, other than what follows from the above.
Results may differ from a plain program's by a relative error of at most 0.003.
Values may be sent and summed in bfloat16 or wider, within the bound.
A program may use at most 64 MiB of HBM per device.

v0:
```python
import functools

import jax
import jax.numpy as jnp
from jax import lax
from jax.experimental import pallas as pl
from jax.experimental.pallas import tpu as pltpu
from jax.sharding import PartitionSpec as P

STEPS = 2
MESH = pl.DeviceIdType.MESH
coupling = 1.5

vectors = (
    (1, 0, 0), (1, 1, 0), (1, -1, 0), (1, 0, 1), (1, 0, -1),
    (-1, 0, 0), (-1, 1, 0), (-1, -1, 0), (-1, 0, 1), (-1, 0, -1),
    (0, 1, 0), (0, -1, 0), (0, 0, 1), (0, 0, -1),
    (0, 1, 1), (0, 1, -1), (0, -1, 1), (0, -1, -1),
    (0, 0, 0),
)
x_lists = tuple(
    ((0, s, 0), (1, s, 0), (-1, s, 0), (0, s, 1), (0, s, -1)) for s in (1, -1)
)
y_lists = tuple(
    ((0, 0, s), (1, 0, s), (-1, 0, s), (0, 1, s), (0, -1, s)) for s in (1, -1)
)
pair_list = ((0, 0), (1, 1), (2, 2), (0, 1), (0, 2), (1, 2))
PAD = 8


def kernel(
    sizes, phase, velocity, stress, sorting, info, out,
    moments, psi, psi_xs, psi_xr, psi_xyr, psi_ys, psi_yr, psi_zy, psi_rows,
    field_a, field_dx, field_dy, field_gx, field_gy,
    pops, pop_xs, pop_xr, pop_xyr, pop_ys, pop_yr, pop_zy,
    sent, arrived, info_in,
    send_sem, recv_sem, move_send, move_recv, info_send, info_recv,
):
    normal, planes, group_z, depth, width, breadth = sizes
    groups = depth // group_z
    me_z = lax.axis_index("normal")
    me_x = lax.axis_index("plane")
    me_y = lax.axis_index("inner")

    def device(offset):
        place = {}
        if offset[0] % normal:
            place["normal"] = lax.rem(me_z + offset[0] % normal, normal)
        if offset[1] % planes:
            place["plane"] = lax.rem(me_x + offset[1] % planes, planes)
        if offset[2] % 2:
            place["inner"] = 1 - me_y
        return place

    around = [
        (0, 0, 1), (1, 0, 0), (-1, 0, 0), (0, 1, 0), (0, -1, 0),
        (1, 0, 1), (-1, 0, 1), (0, 1, 1), (0, -1, 1),
        (1, 1, 0), (-1, 1, 0), (1, -1, 0), (-1, -1, 0),
    ]
    partners = sorted(
        {(a % normal, b % planes, c % 2) for a, b, c in around}
        | {(0, k, 0) for k in range(1, planes)}
    )
    barrier = pltpu.get_barrier_semaphore()
    for offset in partners:
        pl.semaphore_signal(barrier, inc=1, device_id=device(offset), device_id_type=MESH)

    lane = lax.broadcasted_iota(jnp.int32, (width, breadth), 1)
    row = lax.broadcasted_iota(jnp.int32, (width, breadth), 0)
    last = breadth - 1

    def start(kind, step, pairs):
        copies = []
        for number, (offset, (source, target)) in enumerate(zip(around, pairs)):
            copy = pltpu.make_async_remote_copy(
                src_ref=source,
                dst_ref=target,
                send_sem=send_sem.at[kind, step, number],
                recv_sem=recv_sem.at[kind, step, number],
                device_id=device(offset),
                device_id_type=MESH,
            )
            copy.start()
            copies.append(copy)
        return copies

    def from_low_x(value, edge):
        return jnp.where(row == 0, edge, pltpu.roll(value, 1, 0))

    def from_high_x(value, edge):
        return jnp.where(row == width - 1, edge, pltpu.roll(value, width - 1, 0))

    def initial(z, carry):
        density = jnp.where(phase[z] == 1, 2.0, 0.3).astype(jnp.float32)
        speed = [velocity[a, z] for a in range(3)]
        momentum = [density * s for s in speed]
        third = density * (1.0 / 3.0)
        moments[0, z] = density
        for a in range(3):
            moments[1 + a, z] = momentum[a]
        for k, (a, b) in enumerate(pair_list):
            second = momentum[a] * speed[b] + stress[k, z]
            moments[4 + k, z] = second + third if a == b else second
        return carry

    lax.fori_loop(0, depth, initial, 0)
    pl.semaphore_wait(barrier, len(partners))

    info_copies = []
    for k in range(1, planes):
        copy = pltpu.make_async_remote_copy(
            src_ref=info.at[lax.rem(me_x + k, planes)],
            dst_ref=info_in.at[k],
            send_sem=info_send.at[k],
            recv_sem=info_recv.at[k],
            device_id=device((0, k, 0)),
            device_id_type=MESH,
        )
        copy.start()
        info_copies.append(copy)

    def one_step(step, carry):
        def potential(z, packed):
            value = 1.0 - jnp.exp(-moments[0, z])
            psi[step, z + 1] = value
            psi_xs[step, 0, pl.ds(z, 1), :] = value[width - 1 : width]
            psi_xs[step, 1, pl.ds(z, 1), :] = value[0:1]
            packed = jnp.where(lane == z + 17, pltpu.roll(value, z + 18, 1), packed)
            return jnp.where(lane == z + 65, pltpu.roll(value, z + 65, 1), packed)

        psi_ys[step] = lax.fori_loop(
            0, depth, potential, jnp.zeros((width, breadth), jnp.float32)
        )
        low, high = pl.ds(0, PAD), pl.ds(depth - PAD, PAD)
        inner_rows = pl.ds(PAD, depth)
        before, after = pl.ds(0, PAD), pl.ds(depth + PAD, PAD)
        copies = start(0, step, [
            (psi_ys.at[step], psi_yr.at[step]),
            (psi.at[step, depth], psi.at[step, 0]),
            (psi.at[step, 1], psi.at[step, depth + 1]),
            (psi_xs.at[step, 0], psi_xr.at[step, 0, inner_rows]),
            (psi_xs.at[step, 1], psi_xr.at[step, 1, inner_rows]),
            (psi.at[step, depth], psi_zy.at[step, 0]),
            (psi.at[step, 1], psi_zy.at[step, 1]),
            (psi_xs.at[step, 0], psi_xyr.at[step, 0, inner_rows]),
            (psi_xs.at[step, 1], psi_xyr.at[step, 1, inner_rows]),
            (psi_xs.at[step, 0, high], psi_xr.at[step, 0, before]),
            (psi_xs.at[step, 0, low], psi_xr.at[step, 0, after]),
            (psi_xs.at[step, 1, high], psi_xr.at[step, 1, before]),
            (psi_xs.at[step, 1, low], psi_xr.at[step, 1, after]),
        ])
        for copy in copies:
            copy.wait()
        columns = psi_yr[step]
        for side, z_at in ((0, 16), (1, 17 + depth)):
            plane_in = psi_zy[step, side]
            columns = jnp.where(lane == z_at, pltpu.roll(plane_in, z_at + 1, 1), columns)
            columns = jnp.where(lane == z_at + 48, pltpu.roll(plane_in, z_at + 48, 1), columns)
        psi_yr[step] = columns
        rows_lane = lax.broadcasted_iota(jnp.int32, (depth + 2 * PAD, breadth), 1)
        for side in range(2):
            own, other = psi_xr[step, side], psi_xyr[step, side]
            psi_rows[0, side] = pltpu.roll(jnp.where(rows_lane == last, other, own), 1, 1)
            psi_rows[1, side] = pltpu.roll(jnp.where(rows_lane == 0, other, own), last, 1)

        def differences(p, carry):
            value = psi[step, p]
            columns = psi_yr[step]
            at = pl.ds(p + PAD - 1, 1)
            y_low = jnp.where(
                lane == 0, pltpu.roll(columns, 112 - p, 1), pltpu.roll(value, 1, 1)
            )
            y_high = jnp.where(
                lane == last, pltpu.roll(columns, 63 - p, 1), pltpu.roll(value, last, 1)
            )
            y_sum, y_diff = y_high + y_low, y_high - y_low
            x_low = from_low_x(value, psi_xr[step, 0, at, :])
            x_high = from_high_x(value, psi_xr[step, 1, at, :])
            edges = [
                [psi_rows[s, side, at, :] for s in range(2)] for side in range(2)
            ]
            x_diff = x_high - x_low
            field_a[p] = 2.0 * value + (x_high + x_low) + y_sum
            field_dx[p] = x_diff
            field_dy[p] = y_diff
            field_gx[p] = (
                2.0 * x_diff
                + from_high_x(y_sum, edges[1][1] + edges[1][0])
                - from_low_x(y_sum, edges[0][1] + edges[0][0])
            )
            field_gy[p] = (
                2.0 * y_diff
                + from_high_x(y_diff, edges[1][1] - edges[1][0])
                + from_low_x(y_diff, edges[0][1] - edges[0][0])
            )
            return carry

        lax.fori_loop(0, depth + 2, differences, 0)

        def collide(z, packs):
            p = z + 1
            scale = (coupling / 36.0) * psi[step, p]
            force = [
                scale * (field_a[p + 1] - field_a[p - 1]),
                scale * (field_gx[p] + (field_dx[p + 1] + field_dx[p - 1])),
                scale * (field_gy[p] + (field_dy[p + 1] + field_dy[p - 1])),
            ]
            density = moments[0, z]
            inverse = 1.0 / density
            momentum = [moments[1 + a, z] for a in range(3)]
            speed = [m * inverse for m in momentum]
            post = [m + f for m, f in zip(momentum, force)]
            second = {}
            for k, (a, b) in enumerate(pair_list):
                value = (
                    0.625 * (momentum[a] * speed[b])
                    + 0.375 * moments[4 + k, z]
                    + (speed[a] * force[b] + force[a] * speed[b])
                )
                if a == b:
                    second[a, a] = (value - 0.125 * density) * 0.125
                else:
                    second[a, b] = value * 0.25
            flow = [m * (1.0 / 12.0) for m in post]
            base = density * (1.0 / 36.0) - (
                second[0, 0] + second[1, 1] + second[2, 2]
            ) * (1.0 / 3.0)
            value_of = {(0, 0, 0): 12.0 * base}
            for a in range(3):
                even = 2.0 * (base + second[a, a])
                odd = 2.0 * flow[a]
                for sign in (1, -1):
                    vector = [0, 0, 0]
                    vector[a] = sign
                    value_of[tuple(vector)] = even + odd if sign == 1 else even - odd
            for a, b in pair_list[3:]:
                both = base + (second[a, a] + second[b, b])
                for sign in (1, -1):
                    if sign == 1:
                        even, odd = both + second[a, b], flow[a] + flow[b]
                    else:
                        even, odd = both - second[a, b], flow[a] - flow[b]
                    vector = [0, 0, 0]
                    vector[a], vector[b] = 1, sign
                    value_of[tuple(vector)] = even + odd
                    vector[a], vector[b] = -1, -sign
                    value_of[tuple(vector)] = even - odd
            for index, vector in enumerate(vectors):
                pops[step, index, p] = value_of[vector]
            for k in range(5):
                pop_xs[step, 0, k, pl.ds(z, 1), :] = value_of[x_lists[0][k]][width - 1 : width]
                pop_xs[step, 1, k, pl.ds(z, 1), :] = value_of[x_lists[1][k]][0:1]
            up, down = packs
            for k in range(5):
                at = p + 18 * k
                up = jnp.where(lane == at, pltpu.roll(value_of[y_lists[0][k]], at + 1, 1), up)
                down = jnp.where(lane == at, pltpu.roll(value_of[y_lists[1][k]], at, 1), down)
            return up, down

        nothing = jnp.zeros((width, breadth), jnp.float32)
        up, down = lax.fori_loop(0, depth, collide, (nothing, nothing))
        pop_ys[step, 0] = up
        pop_ys[step, 1] = down
        five, two = pl.ds(0, 5), pl.ds(3, 2)
        copies = start(1, step, [
            (pop_ys.at[step], pop_yr.at[step]),
            (pops.at[step, five, depth], pops.at[step, five, 0]),
            (pops.at[step, pl.ds(5, 5), 1], pops.at[step, pl.ds(5, 5), depth + 1]),
            (pop_xs.at[step, 0], pop_xr.at[step, 0, five, inner_rows]),
            (pop_xs.at[step, 1], pop_xr.at[step, 1, five, inner_rows]),
            (pops.at[step, two, depth], pop_zy.at[step, 0]),
            (pops.at[step, pl.ds(8, 2), 1], pop_zy.at[step, 1]),
            (pop_xs.at[step, 0, two], pop_xyr.at[step, 0]),
            (pop_xs.at[step, 1, two], pop_xyr.at[step, 1]),
            (pop_xs.at[step, 0, 1, high], pop_xr.at[step, 0, 1, before]),
            (pop_xs.at[step, 0, 2, low], pop_xr.at[step, 0, 2, after]),
            (pop_xs.at[step, 1, 1, high], pop_xr.at[step, 1, 1, before]),
            (pop_xs.at[step, 1, 2, low], pop_xr.at[step, 1, 2, after]),
        ])
        for copy in copies:
            copy.wait()
        for side in range(2):
            own = pop_xr[step, side, 3, inner_rows, :]
            other = pop_xyr[step, side, 0]
            pop_xr[step, side, 3, inner_rows, :] = pltpu.roll(
                jnp.where(lane == last, other, own), 1, 1
            )
            own = pop_xr[step, side, 4, inner_rows, :]
            other = pop_xyr[step, side, 1]
            pop_xr[step, side, 4, inner_rows, :] = pltpu.roll(
                jnp.where(lane == 0, other, own), last, 1
            )
        far = 36 + depth + 1
        up, down = pop_yr[step, 0], pop_yr[step, 1]
        up = jnp.where(lane == 18, pltpu.roll(pop_zy[step, 0, 0], 19, 1), up)
        down = jnp.where(lane == 18, pltpu.roll(pop_zy[step, 0, 1], 18, 1), down)
        up = jnp.where(lane == far, pltpu.roll(pop_zy[step, 1, 0], far + 1, 1), up)
        down = jnp.where(lane == far, pltpu.roll(pop_zy[step, 1, 1], far, 1), down)
        pop_yr[step, 0] = up
        pop_yr[step, 1] = down

        def stream(z, carry):
            up, down = pop_yr[step, 0], pop_yr[step, 1]
            passed = {}
            for index, vector in enumerate(vectors):
                p = z + 1 - vector[0]
                value = pops[step, index, p]
                if vector[2] == 1:
                    at = p + 18 * y_lists[0].index(vector)
                    value = jnp.where(
                        lane == 0, pltpu.roll(up, 128 - at, 1), pltpu.roll(value, 1, 1)
                    )
                elif vector[2] == -1:
                    at = p + 18 * y_lists[1].index(vector)
                    value = jnp.where(
                        lane == last, pltpu.roll(down, 127 - at, 1), pltpu.roll(value, last, 1)
                    )
                if vector[1] == 1:
                    k = x_lists[0].index(vector)
                    value = from_low_x(value, pop_xr[step, 0, k, pl.ds(p + PAD - 1, 1), :])
                elif vector[1] == -1:
                    k = x_lists[1].index(vector)
                    value = from_high_x(value, pop_xr[step, 1, k, pl.ds(p + PAD - 1, 1), :])
                passed[vector] = value
            totals, moved = {}, {}
            for a in range(3):
                vector = [0, 0, 0]
                vector[a] = 1
                plus = passed[tuple(vector)]
                vector[a] = -1
                minus = passed[tuple(vector)]
                totals[a], moved[a] = plus + minus, plus - minus
            axis_sum = totals[0] + totals[1] + totals[2]
            cross, pair_sum = {}, {}
            for a, b in pair_list[3:]:
                found = {}
                for sign_a in (1, -1):
                    for sign_b in (1, -1):
                        vector = [0, 0, 0]
                        vector[a], vector[b] = sign_a, sign_b
                        found[sign_a, sign_b] = passed[tuple(vector)]
                same = found[1, 1] + found[-1, -1]
                mixed = found[1, -1] + found[-1, 1]
                same_odd = found[1, 1] - found[-1, -1]
                mixed_odd = found[1, -1] - found[-1, 1]
                cross[a, b] = same - mixed
                pair_sum[a, b] = same + mixed
                moved[a] = moved[a] + (same_odd + mixed_odd)
                moved[b] = moved[b] + (same_odd - mixed_odd)
            moments[0, z] = passed[0, 0, 0] + axis_sum + (
                pair_sum[0, 1] + pair_sum[0, 2] + pair_sum[1, 2]
            )
            for a in range(3):
                moments[1 + a, z] = moved[a]
            moments[4, z] = totals[0] + (pair_sum[0, 1] + pair_sum[0, 2])
            moments[5, z] = totals[1] + (pair_sum[0, 1] + pair_sum[1, 2])
            moments[6, z] = totals[2] + (pair_sum[0, 2] + pair_sum[1, 2])
            for k, pair in enumerate(pair_list[3:]):
                moments[7 + k, z] = cross[pair]
            return carry

        lax.fori_loop(0, depth, stream, 0)
        return carry

    lax.fori_loop(0, STEPS, one_step, 0)

    order = sorting[...]
    tile = order.shape[0] // planes
    moves = []
    for g in range(groups):
        def arrange(c, carry):
            block = moments[c, pl.ds(g * group_z, group_z)].reshape(group_z * width, breadth)
            rows = jnp.dot(
                order, block.astype(jnp.bfloat16), preferred_element_type=jnp.float32
            ).astype(jnp.bfloat16)
            sent[g, :, c] = rows.reshape(planes, tile, breadth)
            return carry

        lax.fori_loop(0, 10, arrange, 0)
        for k in range(planes - 1, 0, -1):
            copy = pltpu.make_async_remote_copy(
                src_ref=sent.at[g, lax.rem(me_x + k, planes)],
                dst_ref=arrived.at[g, k],
                send_sem=move_send.at[g, k],
                recv_sem=move_recv.at[g, k],
                device_id=device((0, k, 0)),
                device_id_type=MESH,
            )
            copy.start()
            moves.append((g, copy))
        arrived[g, 0] = sent[g, me_x]

    for copy in info_copies:
        copy.wait()
    slots = planes * tile
    parts = [info[me_x, 0:1, 0:tile]]
    for k in range(1, planes):
        parts.append(info_in[k, 0:1, 0:tile])
    place = jnp.concatenate(parts, axis=1)
    to_row = lax.broadcasted_iota(jnp.int32, (group_z * width, slots), 0)
    from_slot = lax.broadcasted_iota(jnp.int32, (group_z * width, slots), 1)
    capacity = tile // group_z
    fits = (place == lax.rem(to_row, width).astype(jnp.float32)) & (
        lax.rem(from_slot, tile) // capacity == to_row // width
    )
    placing = jnp.where(fits, 1.0, 0.0).astype(jnp.bfloat16)
    for g in range(groups):
        for held, copy in moves:
            if held == g:
                copy.wait()

        def put(c, carry):
            rows = jnp.dot(
                placing,
                arrived[g, :, c].reshape(slots, breadth),
                preferred_element_type=jnp.float32,
            ).astype(jnp.bfloat16)
            out[c, pl.ds(g * group_z, group_z)] = rows.reshape(group_z, width, breadth)
            return carry

        lax.fori_loop(0, 10, put, 0)


def shards(mesh_sizes, phase, velocity, stress, new_slot):
    normal, planes = mesh_sizes
    depth, width, breadth = phase.shape
    capacity = 2 * ((width // 2 + planes - 1) // planes)
    group_z = 16 // capacity
    target = new_slot // width
    position = new_slot % width
    matches = (target[:, None] == jnp.arange(planes, dtype=jnp.int32)[None, :]).astype(jnp.int32)
    earlier = jnp.cumsum(matches, axis=0) - matches
    order_in = jnp.sum(earlier * matches, axis=1)
    slot_index = target * capacity + order_in
    chosen = slot_index[None, :] == jnp.arange(planes * capacity, dtype=jnp.int32)[:, None]
    place = jnp.sum(jnp.where(chosen, position[None, :] + 1, 0), axis=1) - 1
    same = jnp.arange(group_z)[:, None] == jnp.arange(group_z)[None, :]
    sorting = (
        chosen.reshape(planes, 1, capacity, 1, width) & same[None, :, None, :, None]
    ).reshape(planes * 16, group_z * width).astype(jnp.bfloat16)
    info = jnp.tile(place.reshape(planes, 1, capacity), (1, group_z, 1)).reshape(planes, 1, 16)
    info = jnp.pad(
        jnp.broadcast_to(info, (planes, 8, 16)).astype(jnp.float32),
        ((0, 0), (0, 0), (0, 112)),
    )
    groups = depth // group_z
    plane = (width, breadth)
    padded = (depth + 2 * PAD, breadth)
    f32, bf16 = jnp.float32, jnp.bfloat16
    vmem = pltpu.VMEM
    dma = pltpu.SemaphoreType.DMA
    whole = pl.BlockSpec(memory_space=pltpu.VMEM)
    return pl.pallas_call(
        functools.partial(kernel, (normal, planes, group_z, depth, width, breadth)),
        out_shape=jax.ShapeDtypeStruct((10, depth, width, breadth), bf16),
        in_specs=[whole] * 5,
        out_specs=whole,
        scratch_shapes=[
            vmem((10, depth) + plane, f32),
            vmem((STEPS, depth + 2) + plane, f32),
            vmem((STEPS, 2, depth, breadth), f32),
            vmem((STEPS, 2) + padded, f32),
            vmem((STEPS, 2) + padded, f32),
            vmem((STEPS,) + plane, f32),
            vmem((STEPS,) + plane, f32),
            vmem((STEPS, 2) + plane, f32),
            vmem((2, 2) + padded, f32),
        ]
        + [vmem((depth + 2,) + plane, f32)] * 5
        + [
            vmem((STEPS, 19, depth + 2) + plane, f32),
            vmem((STEPS, 2, 5, depth, breadth), f32),
            vmem((STEPS, 2, 5) + padded, f32),
            vmem((STEPS, 2, 2, depth, breadth), f32),
            vmem((STEPS, 2) + plane, f32),
            vmem((STEPS, 2) + plane, f32),
            vmem((STEPS, 2, 2) + plane, f32),
            vmem((groups, planes, 10, 16, breadth), bf16),
            vmem((groups, planes, 10, 16, breadth), bf16),
            vmem((planes, 8, 128), f32),
            dma((2, STEPS, 13)),
            dma((2, STEPS, 13)),
            dma((groups, planes)),
            dma((groups, planes)),
            dma((planes,)),
            dma((planes,)),
        ],
        compiler_params=pltpu.CompilerParams(
            collective_id=0, has_side_effects=True, vmem_limit_bytes=40 * 1024 * 1024
        ),
    )(phase, velocity, stress, sorting, info)


def solution(mesh):
    placed = (
        P(("groups", "normal"), "plane", "inner"),
        P(None, ("groups", "normal"), "plane", "inner"),
        P(None, ("groups", "normal"), "plane", "inner"),
        P(("groups", "plane")),
    )
    return jax.shard_map(
        functools.partial(shards, (mesh.shape["normal"], mesh.shape["plane"])),
        mesh=mesh,
        in_specs=placed,
        out_specs=P(None, ("groups", "normal"), "plane", "inner"),
        check_vma=False,
    )
```

profile of v0, /device:TPU:0, one launch (start us, length us, event | category | flops | bytes accessed | tf_op | source)
XLA Modules:
  0.0 63.0 jit_solution(15690563946059890666)
XLA Ops:
  0.0 0.0 copy-start.3
  0.0 0.6 %copy-done.3 = s32[16]{0:T(128)S(1)} copy-done((s32[16]{0:T(128)S(1)}, s32[16]{0:T(128)}, u32[]{:S(2)}) %copy-start.3) | copy-done | bytes 88
  0.7 0.1 fusion
  0.8 0.0 copy-start.2
  0.8 0.2 select_reduce_fusion.1
  1.0 0.1 select_reduce_fusion
  1.1 0.1 broadcast_compare_fusion
  1.2 0.1 convert_element_type.25
  1.3 0.1 convert_element_type.26
  1.4 0.1 and_convert_fusion
  1.5 0.1 reshape.55.sorting
  1.6 0.1 copy-done.2
  1.7 0.0 copy-start
  1.7 1.1 %copy-done = f32[6,16,16,128]{3,2,1,0:T(8,128)S(1)} copy-done((f32[6,16,16,128]{3,2,1,0:T(8,128)S(1)}, f32[6,16,16,128]{3,2,1,0:T(8,128)}, u32[]{:S(2)}) %copy-start) | copy-done | bytes 786456
  2.8 0.0 copy-start.1
  2.8 1.0 %copy-done.1 = f32[3,16,16,128]{3,2,1,0:T(8,128)S(1)} copy-done((f32[3,16,16,128]{3,2,1,0:T(8,128)S(1)}, f32[3,16,16,128]{3,2,1,0:T(8,128)}, u32[]{:S(2)}) %copy-start.1) | copy-done | bytes 393240
  3.8 58.3 %shard_map.46 = bf16[10,16,16,128]{3,2,1,0:T(8,128)(2,1)S(1)} custom-call(s32[16,16,128]{2,1,0:T(8,128)S(1)} %copy-done.2, f32[3,16,16,128]{3,2,1,0:T(8,128)S(1)} %copy-done.1, f32[6,16,16,128]{3,2,1,0:T(8,128)S(1)} %copy-done, bf16[64,64]{1,0:T(8,128)(2,1)S(1)} %reshape.55.sorting, f32[4,8,128]{2,1,0:T(8,128)S(1)} %pad.4.info), custom_call_target="tpu_custom_call" | custom-call | tf_op jit(solution)/shard_map/pallas_call | solution.py:453
  62.1 0.8 %copy.6 = bf16[10,16,16,128]{3,2,1,0:T(8,128)(2,1)} copy(bf16[10,16,16,128]{3,2,1,0:T(8,128)(2,1)S(1)} %shard_map.46) | data formatting | bytes 1310720
  (9 shorter events, 0.1 us)
Async XLA Ops:
  0.0 0.7 %copy-start.3 = (s32[16]{0:T(128)S(1)}, s32[16]{0:T(128)}, u32[]{:S(2)}) copy-start(s32[16]{0:T(128)} %param.7) | copy-start | bytes 196
  0.8 0.9 %copy-start.2 = (s32[16,16,128]{2,1,0:T(8,128)S(1)}, s32[16,16,128]{2,1,0:T(8,128)}, u32[]{:S(2)}) copy-start(s32[16,16,128]{2,1,0:T(8,128)} %phase.1) | copy-start | bytes 393220
  1.7 1.1 %copy-start = (f32[6,16,16,128]{3,2,1,0:T(8,128)S(1)}, f32[6,16,16,128]{3,2,1,0:T(8,128)}, u32[]{:S(2)}) copy-start(f32[6,16,16,128]{3,2,1,0:T(8,128)} %stress.1) | copy-start | bytes 2359300
  2.8 1.0 %copy-start.1 = (f32[3,16,16,128]{3,2,1,0:T(8,128)S(1)}, f32[3,16,16,128]{3,2,1,0:T(8,128)}, u32[]{:S(2)}) copy-start(f32[3,16,16,128]{3,2,1,0:T(8,128)} %velocity.1) | copy-start | bytes 1179652
where the time goes:
time: 63.2 us; the launch traced here: 63 us
  Pallas kernels  58.3 us (92%)
  local copies, waits for them, and re-layouts  3.97 us (6%)
    pallas_call x1, Pallas kernels, shards(): pl.pallas_call(functools.partial(kernel, (normal, planes, group_z, depth,...  58.3 us
    unnamed x9, local copies, waits for them, and re-layouts  3.68 us

commit v1 on v0

--- a/solution.py
+++ b/solution.py
@@ -29,12 +29,12 @@
 
 
 def kernel(
-    sizes, phase, velocity, stress, sorting, info, out,
-    moments, psi, psi_xs, psi_xr, psi_xyr, psi_ys, psi_yr, psi_zy, psi_rows,
+    sizes, phase_hbm, velocity_hbm, stress_hbm, new_slot, out,
+    phase, velocity, stress, moments, speeds, psi, psi_xs, psi_xr, psi_xyr, psi_ys, psi_yr, psi_zy, psi_rows,
     field_a, field_dx, field_dy, field_gx, field_gy,
-    pops, pop_xs, pop_xr, pop_xyr, pop_ys, pop_yr, pop_zy,
-    sent, arrived, info_in,
-    send_sem, recv_sem, move_send, move_recv, info_send, info_recv,
+    pops, pop_rows, pop_xs, pop_xin, pop_xyr, pop_zxr, pop_ys, pop_yr,
+    pop_zs, pop_zin, pop_zy, side_sums, sent, arrived, info, info_in,
+    load_sem, send_sem, recv_sem, move_send, move_recv, info_send, info_recv,
 ):
     normal, planes, group_z, depth, width, breadth = sizes
     groups = depth // group_z
@@ -61,6 +61,14 @@
         {(a % normal, b % planes, c % 2) for a, b, c in around}
         | {(0, k, 0) for k in range(1, planes)}
     )
+    loads = [
+        pltpu.make_async_copy(source, target, load_sem.at[number])
+        for number, (source, target) in enumerate(
+            ((phase_hbm, phase), (velocity_hbm, velocity), (stress_hbm, stress))
+        )
+    ]
+    for load in loads:
+        load.start()
     barrier = pltpu.get_barrier_semaphore()
     for offset in partners:
         pl.semaphore_signal(barrier, inc=1, device_id=device(offset), device_id_type=MESH)
@@ -91,35 +99,83 @@
         return jnp.where(row == width - 1, edge, pltpu.roll(value, width - 1, 0))
 
     def initial(z, carry):
-        density = jnp.where(phase[z] == 1, 2.0, 0.3).astype(jnp.float32)
+        density = moments[0, z]
         speed = [velocity[a, z] for a in range(3)]
         momentum = [density * s for s in speed]
-        third = density * (1.0 / 3.0)
-        moments[0, z] = density
         for a in range(3):
             moments[1 + a, z] = momentum[a]
+            speeds[a, z] = speed[a]
         for k, (a, b) in enumerate(pair_list):
-            second = momentum[a] * speed[b] + stress[k, z]
-            moments[4 + k, z] = second + third if a == b else second
+            moments[4 + k, z] = momentum[a] * speed[b] + 0.375 * stress[k, z]
         return carry
 
-    lax.fori_loop(0, depth, initial, 0)
-    pl.semaphore_wait(barrier, len(partners))
-
+    def prepare(z, carry):
+        density = moments[0, z]
+        inverse = 1.0 / density
+        momentum = [moments[1 + a, z] for a in range(3)]
+        speed = [m * inverse for m in momentum]
+        eighth = 0.125 * density
+        for a in range(3):
+            speeds[a, z] = speed[a]
+        for k, (a, b) in enumerate(pair_list):
+            value = 0.625 * (momentum[a] * speed[b]) + 0.375 * moments[4 + k, z]
+            moments[4 + k, z] = value - eighth if a == b else value
+        return carry
+
+    def start_density(z, carry):
+        moments[0, z] = jnp.where(phase[z] == 1, 2.0, 0.3).astype(jnp.float32)
+        return carry
+
+    loads[0].wait()
+    lax.fori_loop(0, depth, start_density, 0, unroll=4)
+
+    tile = 16
+    capacity = tile // group_z
     info_copies = []
-    for k in range(1, planes):
-        copy = pltpu.make_async_remote_copy(
-            src_ref=info.at[lax.rem(me_x + k, planes)],
-            dst_ref=info_in.at[k],
-            send_sem=info_send.at[k],
-            recv_sem=info_recv.at[k],
-            device_id=device((0, k, 0)),
-            device_id_type=MESH,
-        )
-        copy.start()
-        info_copies.append(copy)
-
-    def one_step(step, carry):
+
+    def plan():
+        slots = planes * tile
+        blocks = [new_slot[x] for x in range(width)]
+        owners = [lax.div(block, width) for block in blocks]
+        places = [lax.rem(block, width) for block in blocks]
+        at_slot = []
+        for x in range(width):
+            earlier = jnp.int32(0)
+            for other in range(x):
+                earlier = earlier + jnp.where(owners[other] == owners[x], 1, 0)
+            at_slot.append(owners[x] * capacity + earlier)
+        shape = (slots, group_z * width)
+        to_slot = lax.broadcasted_iota(jnp.int32, shape, 0)
+        from_cell = lax.broadcasted_iota(jnp.int32, shape, 1)
+        from_x = lax.rem(from_cell[0:8], width)
+        slot_of = jnp.zeros(from_x.shape, jnp.int32)
+        for x in range(width):
+            slot_of = jnp.where(from_x == x, at_slot[x], slot_of)
+        here = lax.div(to_slot, tile) * capacity + lax.rem(to_slot, capacity)
+        layer = lax.div(lax.rem(to_slot, tile), capacity)
+        chosen = (slot_of[0:1] == here) & (layer == lax.div(from_cell, width))
+        order = jnp.where(chosen, 1.0, 0.0).astype(jnp.bfloat16)
+        small = lax.broadcasted_iota(jnp.int32, (8, 128), 1)
+        for t in range(planes):
+            wanted = lax.rem(small, capacity) + t * capacity
+            place = jnp.full((8, 128), -1, jnp.int32)
+            for x in range(width):
+                place = jnp.where(wanted == at_slot[x], places[x], place)
+            info[t] = place.astype(jnp.float32)
+        for k in range(1, planes):
+            copy = pltpu.make_async_remote_copy(
+                src_ref=info.at[lax.rem(me_x + k, planes)],
+                dst_ref=info_in.at[k],
+                send_sem=info_send.at[k],
+                recv_sem=info_recv.at[k],
+                device_id=device((0, k, 0)),
+                device_id_type=MESH,
+            )
+            copy.start()
+            info_copies.append(copy)
+        return order
+
+    for step in range(STEPS):
         def potential(z, packed):
             value = 1.0 - jnp.exp(-moments[0, z])
             psi[step, z + 1] = value
@@ -129,11 +185,13 @@
             return jnp.where(lane == z + 65, pltpu.roll(value, z + 65, 1), packed)
 
         psi_ys[step] = lax.fori_loop(
-            0, depth, potential, jnp.zeros((width, breadth), jnp.float32)
+            0, depth, potential, jnp.zeros((width, breadth), jnp.float32), unroll=4
         )
         low, high = pl.ds(0, PAD), pl.ds(depth - PAD, PAD)
         inner_rows = pl.ds(PAD, depth)
         before, after = pl.ds(0, PAD), pl.ds(depth + PAD, PAD)
+        if step == 0:
+            pl.semaphore_wait(barrier, len(partners))
         copies = start(0, step, [
             (psi_ys.at[step], psi_yr.at[step]),
             (psi.at[step, depth], psi.at[step, 0]),
@@ -149,6 +207,13 @@
             (psi_xs.at[step, 1, high], psi_xr.at[step, 1, before]),
             (psi_xs.at[step, 1, low], psi_xr.at[step, 1, after]),
         ])
+        if step == 0:
+            order = plan()
+            loads[1].wait()
+            loads[2].wait()
+            lax.fori_loop(0, depth, initial, 0)
+        else:
+            lax.fori_loop(0, depth, prepare, 0)
         for copy in copies:
             copy.wait()
         columns = psi_yr[step]
@@ -195,7 +260,7 @@
             )
             return carry
 
-        lax.fori_loop(0, depth + 2, differences, 0)
+        lax.fori_loop(0, depth + 2, differences, 0, unroll=2)
 
         def collide(z, packs):
             p = z + 1
@@ -206,21 +271,13 @@
                 scale * (field_gy[p] + (field_dy[p + 1] + field_dy[p - 1])),
             ]
             density = moments[0, z]
-            inverse = 1.0 / density
             momentum = [moments[1 + a, z] for a in range(3)]
-            speed = [m * inverse for m in momentum]
+            speed = [speeds[a, z] for a in range(3)]
             post = [m + f for m, f in zip(momentum, force)]
             second = {}
             for k, (a, b) in enumerate(pair_list):
-                value = (
-                    0.625 * (momentum[a] * speed[b])
-                    + 0.375 * moments[4 + k, z]
-                    + (speed[a] * force[b] + force[a] * speed[b])
-                )
-                if a == b:
-                    second[a, a] = (value - 0.125 * density) * 0.125
-                else:
-                    second[a, b] = value * 0.25
+                value = moments[4 + k, z] + (speed[a] * force[b] + force[a] * speed[b])
+                second[a, b] = value * (0.125 if a == b else 0.25)
             flow = [m * (1.0 / 12.0) for m in post]
             base = density * (1.0 / 36.0) - (
                 second[0, 0] + second[1, 1] + second[2, 2]
@@ -248,8 +305,8 @@
             for index, vector in enumerate(vectors):
                 pops[step, index, p] = value_of[vector]
             for k in range(5):
-                pop_xs[step, 0, k, pl.ds(z, 1), :] = value_of[x_lists[0][k]][width - 1 : width]
-                pop_xs[step, 1, k, pl.ds(z, 1), :] = value_of[x_lists[1][k]][0:1]
+                pop_rows[0, k, pl.ds(z, 1), :] = value_of[x_lists[0][k]][width - 1 : width]
+                pop_rows[1, k, pl.ds(z, 1), :] = value_of[x_lists[1][k]][0:1]
             up, down = packs
             for k in range(5):
                 at = p + 18 * k
@@ -261,43 +318,27 @@
         up, down = lax.fori_loop(0, depth, collide, (nothing, nothing))
         pop_ys[step, 0] = up
         pop_ys[step, 1] = down
-        five, two = pl.ds(0, 5), pl.ds(3, 2)
+        for k in range(5):
+            pop_zs[step, 0, k] = pops[step, k, depth].astype(jnp.bfloat16)
+            pop_zs[step, 1, k] = pops[step, 5 + k, 1].astype(jnp.bfloat16)
+            for side in range(2):
+                pop_xs[step, side, k] = pop_rows[side, k].astype(jnp.bfloat16)
+        two = pl.ds(3, 2)
         copies = start(1, step, [
             (pop_ys.at[step], pop_yr.at[step]),
-            (pops.at[step, five, depth], pops.at[step, five, 0]),
-            (pops.at[step, pl.ds(5, 5), 1], pops.at[step, pl.ds(5, 5), depth + 1]),
-            (pop_xs.at[step, 0], pop_xr.at[step, 0, five, inner_rows]),
-            (pop_xs.at[step, 1], pop_xr.at[step, 1, five, inner_rows]),
-            (pops.at[step, two, depth], pop_zy.at[step, 0]),
-            (pops.at[step, pl.ds(8, 2), 1], pop_zy.at[step, 1]),
+            (pop_zs.at[step, 0], pop_zin.at[step, 0]),
+            (pop_zs.at[step, 1], pop_zin.at[step, 1]),
+            (pop_xs.at[step, 0], pop_xin.at[step, 0]),
+            (pop_xs.at[step, 1], pop_xin.at[step, 1]),
+            (pop_zs.at[step, 0, two], pop_zy.at[step, 0]),
+            (pop_zs.at[step, 1, two], pop_zy.at[step, 1]),
             (pop_xs.at[step, 0, two], pop_xyr.at[step, 0]),
             (pop_xs.at[step, 1, two], pop_xyr.at[step, 1]),
-            (pop_xs.at[step, 0, 1, high], pop_xr.at[step, 0, 1, before]),
-            (pop_xs.at[step, 0, 2, low], pop_xr.at[step, 0, 2, after]),
-            (pop_xs.at[step, 1, 1, high], pop_xr.at[step, 1, 1, before]),
-            (pop_xs.at[step, 1, 2, low], pop_xr.at[step, 1, 2, after]),
+            (pop_xs.at[step, 0, 1], pop_zxr.at[step, 0, 0]),
+            (pop_xs.at[step, 0, 2], pop_zxr.at[step, 0, 1]),
+            (pop_xs.at[step, 1, 1], pop_zxr.at[step, 1, 0]),
+            (pop_xs.at[step, 1, 2], pop_zxr.at[step, 1, 1]),
         ])
-        for copy in copies:
-            copy.wait()
-        for side in range(2):
-            own = pop_xr[step, side, 3, inner_rows, :]
-            other = pop_xyr[step, side, 0]
-            pop_xr[step, side, 3, inner_rows, :] = pltpu.roll(
-                jnp.where(lane == last, other, own), 1, 1
-            )
-            own = pop_xr[step, side, 4, inner_rows, :]
-            other = pop_xyr[step, side, 1]
-            pop_xr[step, side, 4, inner_rows, :] = pltpu.roll(
-                jnp.where(lane == 0, other, own), last, 1
-            )
-        far = 36 + depth + 1
-        up, down = pop_yr[step, 0], pop_yr[step, 1]
-        up = jnp.where(lane == 18, pltpu.roll(pop_zy[step, 0, 0], 19, 1), up)
-        down = jnp.where(lane == 18, pltpu.roll(pop_zy[step, 0, 1], 18, 1), down)
-        up = jnp.where(lane == far, pltpu.roll(pop_zy[step, 1, 0], far + 1, 1), up)
-        down = jnp.where(lane == far, pltpu.roll(pop_zy[step, 1, 1], far, 1), down)
-        pop_yr[step, 0] = up
-        pop_yr[step, 1] = down
 
         def stream(z, carry):
             up, down = pop_yr[step, 0], pop_yr[step, 1]
@@ -316,11 +357,9 @@
                         lane == last, pltpu.roll(down, 127 - at, 1), pltpu.roll(value, last, 1)
                     )
                 if vector[1] == 1:
-                    k = x_lists[0].index(vector)
-                    value = from_low_x(value, pop_xr[step, 0, k, pl.ds(p + PAD - 1, 1), :])
+                    value = from_low_x(value, 0.0)
                 elif vector[1] == -1:
-                    k = x_lists[1].index(vector)
-                    value = from_high_x(value, pop_xr[step, 1, k, pl.ds(p + PAD - 1, 1), :])
+                    value = from_high_x(value, 0.0)
                 passed[vector] = value
             totals, moved = {}, {}
             for a in range(3):
@@ -359,24 +398,78 @@
                 moments[7 + k, z] = cross[pair]
             return carry
 
-        lax.fori_loop(0, depth, stream, 0)
-        return carry
-
-    lax.fori_loop(0, STEPS, one_step, 0)
-
-    order = sorting[...]
-    tile = order.shape[0] // planes
+        copies[0].wait()
+        lax.fori_loop(1, depth - 1, stream, 0)
+        for copy in copies[1:]:
+            copy.wait()
+        f32 = jnp.float32
+        for k in range(5):
+            pops[step, k, 0] = pop_zin[step, 0, k].astype(f32)
+            pops[step, 5 + k, depth + 1] = pop_zin[step, 1, k].astype(f32)
+        far = 36 + depth + 1
+        corner = [[pop_zy[step, side, k].astype(f32) for k in range(2)] for side in range(2)]
+        up, down = pop_yr[step, 0], pop_yr[step, 1]
+        up = jnp.where(lane == 18, pltpu.roll(corner[0][0], 19, 1), up)
+        down = jnp.where(lane == 18, pltpu.roll(corner[0][1], 18, 1), down)
+        up = jnp.where(lane == far, pltpu.roll(corner[1][0], far + 1, 1), up)
+        down = jnp.where(lane == far, pltpu.roll(corner[1][1], far, 1), down)
+        pop_yr[step, 0] = up
+        pop_yr[step, 1] = down
+        lax.fori_loop(0, 2, lambda i, carry: stream(i * (depth - 1), carry), 0)
+
+        z_row = lax.broadcasted_iota(jnp.int32, (depth, breadth), 0)
+        z_lane = lax.broadcasted_iota(jnp.int32, (depth, breadth), 1)
+        for side in range(2):
+            own = [pop_xin[step, side, k].astype(f32) for k in range(5)]
+            edge = [pop_zxr[step, side, k].astype(f32) for k in range(2)]
+            other = [pop_xyr[step, side, k].astype(f32) for k in range(2)]
+            plain = own[0]
+            z_up = jnp.where(z_row == 0, pltpu.roll(edge[0], 1, 0), pltpu.roll(own[1], 1, 0))
+            z_down = jnp.where(
+                z_row == depth - 1,
+                pltpu.roll(edge[1], depth - 1, 0),
+                pltpu.roll(own[2], depth - 1, 0),
+            )
+            y_up = pltpu.roll(jnp.where(z_lane == last, other[0], own[3]), 1, 1)
+            y_down = pltpu.roll(jnp.where(z_lane == 0, other[1], own[4]), last, 1)
+            z_even, z_odd = z_up + z_down, z_up - z_down
+            y_even, y_odd = y_up + y_down, y_up - y_down
+            total = plain + (z_even + y_even)
+            if side == 0:
+                adds = [total, z_odd, total, y_odd, z_even, total, y_even, z_odd, y_odd]
+            else:
+                adds = [total, z_odd, -total, y_odd, z_even, total, y_even, -z_odd, -y_odd]
+            for k, add in enumerate(adds):
+                side_sums[side, k] = add
+
+        def add_sides(z, carry):
+            at = pl.ds(z, 1)
+            for k, c in enumerate((0, 1, 2, 3, 4, 5, 6, 7, 9)):
+                for side, x in ((0, 0), (1, width - 1)):
+                    cells = (c, z, pl.ds(x, 1), slice(None))
+                    moments[cells] = moments[cells] + side_sums[side, k, at, :]
+            return carry
+
+        if step < STEPS - 1:
+            lax.fori_loop(0, depth, add_sides, 0)
+
     moves = []
     for g in range(groups):
-        def arrange(c, carry):
-            block = moments[c, pl.ds(g * group_z, group_z)].reshape(group_z * width, breadth)
-            rows = jnp.dot(
-                order, block.astype(jnp.bfloat16), preferred_element_type=jnp.float32
-            ).astype(jnp.bfloat16)
-            sent[g, :, c] = rows.reshape(planes, tile, breadth)
-            return carry
-
-        lax.fori_loop(0, 10, arrange, 0)
+        lax.fori_loop(g * group_z, (g + 1) * group_z, add_sides, 0)
+        block = jnp.concatenate(
+            [
+                moments[c, g * group_z : (g + 1) * group_z]
+                .reshape(group_z * width, breadth)
+                .astype(jnp.bfloat16)
+                for c in range(10)
+            ],
+            axis=1,
+        )
+        rows = jnp.dot(order, block, preferred_element_type=jnp.float32).astype(jnp.bfloat16)
+        for c in range(10):
+            sent[g, :, c] = rows[:, c * breadth : (c + 1) * breadth].reshape(
+                planes, tile, breadth
+            )
         for k in range(planes - 1, 0, -1):
             copy = pltpu.make_async_remote_copy(
                 src_ref=sent.at[g, lax.rem(me_x + k, planes)],
@@ -399,7 +492,6 @@
     place = jnp.concatenate(parts, axis=1)
     to_row = lax.broadcasted_iota(jnp.int32, (group_z * width, slots), 0)
     from_slot = lax.broadcasted_iota(jnp.int32, (group_z * width, slots), 1)
-    capacity = tile // group_z
     fits = (place == lax.rem(to_row, width).astype(jnp.float32)) & (
         lax.rem(from_slot, tile) // capacity == to_row // width
     )
@@ -409,16 +501,14 @@
             if held == g:
                 copy.wait()
 
-        def put(c, carry):
-            rows = jnp.dot(
-                placing,
-                arrived[g, :, c].reshape(slots, breadth),
-                preferred_element_type=jnp.float32,
-            ).astype(jnp.bfloat16)
-            out[c, pl.ds(g * group_z, group_z)] = rows.reshape(group_z, width, breadth)
-            return carry
-
-        lax.fori_loop(0, 10, put, 0)
+        block = jnp.concatenate(
+            [arrived[g, :, c].reshape(slots, breadth) for c in range(10)], axis=1
+        )
+        rows = jnp.dot(placing, block, preferred_element_type=jnp.float32).astype(jnp.bfloat16)
+        for c in range(10):
+            out[c, pl.ds(g * group_z, group_z)] = rows[
+                :, c * breadth : (c + 1) * breadth
+            ].reshape(group_z, width, breadth)
 
 
 def shards(mesh_sizes, phase, velocity, stress, new_slot):
@@ -426,23 +516,6 @@
     depth, width, breadth = phase.shape
     capacity = 2 * ((width // 2 + planes - 1) // planes)
     group_z = 16 // capacity
-    target = new_slot // width
-    position = new_slot % width
-    matches = (target[:, None] == jnp.arange(planes, dtype=jnp.int32)[None, :]).astype(jnp.int32)
-    earlier = jnp.cumsum(matches, axis=0) - matches
-    order_in = jnp.sum(earlier * matches, axis=1)
-    slot_index = target * capacity + order_in
-    chosen = slot_index[None, :] == jnp.arange(planes * capacity, dtype=jnp.int32)[:, None]
-    place = jnp.sum(jnp.where(chosen, position[None, :] + 1, 0), axis=1) - 1
-    same = jnp.arange(group_z)[:, None] == jnp.arange(group_z)[None, :]
-    sorting = (
-        chosen.reshape(planes, 1, capacity, 1, width) & same[None, :, None, :, None]
-    ).reshape(planes * 16, group_z * width).astype(jnp.bfloat16)
-    info = jnp.tile(place.reshape(planes, 1, capacity), (1, group_z, 1)).reshape(planes, 1, 16)
-    info = jnp.pad(
-        jnp.broadcast_to(info, (planes, 8, 16)).astype(jnp.float32),
-        ((0, 0), (0, 0), (0, 112)),
-    )
     groups = depth // group_z
     plane = (width, breadth)
     padded = (depth + 2 * PAD, breadth)
@@ -453,10 +526,15 @@
     return pl.pallas_call(
         functools.partial(kernel, (normal, planes, group_z, depth, width, breadth)),
         out_shape=jax.ShapeDtypeStruct((10, depth, width, breadth), bf16),
-        in_specs=[whole] * 5,
+        in_specs=[pl.BlockSpec(memory_space=pltpu.HBM)] * 3
+        + [pl.BlockSpec(memory_space=pltpu.SMEM)],
         out_specs=whole,
         scratch_shapes=[
+            vmem((depth,) + plane, jnp.int32),
+            vmem((3, depth) + plane, f32),
+            vmem((6, depth) + plane, f32),
             vmem((10, depth) + plane, f32),
+            vmem((3, depth) + plane, f32),
             vmem((STEPS, depth + 2) + plane, f32),
             vmem((STEPS, 2, depth, breadth), f32),
             vmem((STEPS, 2) + padded, f32),
@@ -469,15 +547,22 @@
         + [vmem((depth + 2,) + plane, f32)] * 5
         + [
             vmem((STEPS, 19, depth + 2) + plane, f32),
-            vmem((STEPS, 2, 5, depth, breadth), f32),
-            vmem((STEPS, 2, 5) + padded, f32),
-            vmem((STEPS, 2, 2, depth, breadth), f32),
+            vmem((2, 5, depth, breadth), f32),
+            vmem((STEPS, 2, 5, depth, breadth), bf16),
+            vmem((STEPS, 2, 5, depth, breadth), bf16),
+            vmem((STEPS, 2, 2, depth, breadth), bf16),
+            vmem((STEPS, 2, 2, depth, breadth), bf16),
             vmem((STEPS, 2) + plane, f32),
             vmem((STEPS, 2) + plane, f32),
-            vmem((STEPS, 2, 2) + plane, f32),
+            vmem((STEPS, 2, 5) + plane, bf16),
+            vmem((STEPS, 2, 5) + plane, bf16),
+            vmem((STEPS, 2, 2) + plane, bf16),
+            vmem((2, 9, depth, breadth), f32),
             vmem((groups, planes, 10, 16, breadth), bf16),
             vmem((groups, planes, 10, 16, breadth), bf16),
             vmem((planes, 8, 128), f32),
+            vmem((planes, 8, 128), f32),
+            dma((3,)),
             dma((2, STEPS, 13)),
             dma((2, STEPS, 13)),
             dma((groups, planes)),
@@ -488,7 +573,7 @@
         compiler_params=pltpu.CompilerParams(
             collective_id=0, has_side_effects=True, vmem_limit_bytes=40 * 1024 * 1024
         ),
-    )(phase, velocity, stress, sorting, info)
+    )(phase, velocity, stress, new_slot)
 
 
 def solution(mesh):

time: 63.2 us -> 52.9 us (0.84)
  Pallas kernels: 58.3 us -> 48.2 us
    pallas_call x1, Pallas kernels: 58.3 us -> 48.2 us  [shards(): pl.pallas_call(functools.partial(kernel, (normal, planes, group_z, depth,...]
    unnamed x9, local copies, waits for them, and re-layouts: 3.68 us -> 4.53 us
where the time goes in v1:
time: 52.9 us; the launch traced here: 52.7 us
  Pallas kernels  48.2 us (91%)
  local copies, waits for them, and re-layouts  4.53 us (9%)
    pallas_call x1, Pallas kernels, shards(): pl.pallas_call(functools.partial(kernel, (normal, planes, group_z, depth,...  48.2 us
    unnamed x9, local copies, waits for them, and re-layouts  4.53 us

profile of v1, /device:TPU:0, one launch (start us, length us, event | category | flops | bytes accessed | tf_op | source)
XLA Modules:
  0.0 52.7 jit_solution(5066790767139550860)
XLA Ops:
  0.0 0.0 copy-start
  0.0 1.1 %copy-done = f32[6,16,16,128]{3,2,1,0:T(8,128)S(1)} copy-done((f32[6,16,16,128]{3,2,1,0:T(8,128)S(1)}, f32[6,16,16,128]{3,2,1,0:T(8,128)}, u32[]{:S(2)}) %copy-start) | copy-done | bytes 786456
  1.1 0.0 copy-start.1
  1.1 1.0 %copy-done.1 = f32[3,16,16,128]{3,2,1,0:T(8,128)S(1)} copy-done((f32[3,16,16,128]{3,2,1,0:T(8,128)S(1)}, f32[3,16,16,128]{3,2,1,0:T(8,128)}, u32[]{:S(2)}) %copy-start.1) | copy-done | bytes 393240
  2.1 0.0 copy-start.2
  2.1 0.9 %copy-done.2 = s32[16,16,128]{2,1,0:T(8,128)S(1)} copy-done((s32[16,16,128]{2,1,0:T(8,128)S(1)}, s32[16,16,128]{2,1,0:T(8,128)}, u32[]{:S(2)}) %copy-start.2) | copy-done | bytes 131096
  3.0 0.0 copy-start.3
  3.0 0.7 %copy-done.3 = s32[16]{0:T(128)S(1)} copy-done((s32[16]{0:T(128)S(1)}, s32[16]{0:T(128)}, u32[]{:S(2)}) %copy-start.3) | copy-done | bytes 88
  3.7 48.2 %shard_map.46 = bf16[10,16,16,128]{3,2,1,0:T(8,128)(2,1)S(1)} custom-call(s32[16,16,128]{2,1,0:T(8,128)S(1)} %copy-done.2, f32[3,16,16,128]{3,2,1,0:T(8,128)S(1)} %copy-done.1, f32[6,16,16,128]{3,2,1,0:T(8,128)S(1)} %copy-done, s32[16]{0:T(128)S(1)} %copy-done.3), custom_call_target="tpu_custom_call" | custom-call | tf_op jit(solution)/shard_map/pallas_call | solution.py:526
  51.9 0.8 %copy.6 = bf16[10,16,16,128]{3,2,1,0:T(8,128)(2,1)} copy(bf16[10,16,16,128]{3,2,1,0:T(8,128)(2,1)S(1)} %shard_map.46) | data formatting | bytes 1310720
Async XLA Ops:
  0.0 1.1 %copy-start = (f32[6,16,16,128]{3,2,1,0:T(8,128)S(1)}, f32[6,16,16,128]{3,2,1,0:T(8,128)}, u32[]{:S(2)}) copy-start(f32[6,16,16,128]{3,2,1,0:T(8,128)} %stress_hbm.1) | copy-start | bytes 2359300
  1.1 1.0 %copy-start.1 = (f32[3,16,16,128]{3,2,1,0:T(8,128)S(1)}, f32[3,16,16,128]{3,2,1,0:T(8,128)}, u32[]{:S(2)}) copy-start(f32[3,16,16,128]{3,2,1,0:T(8,128)} %velocity_hbm.1) | copy-start | bytes 1179652
  2.1 0.9 %copy-start.2 = (s32[16,16,128]{2,1,0:T(8,128)S(1)}, s32[16,16,128]{2,1,0:T(8,128)}, u32[]{:S(2)}) copy-start(s32[16,16,128]{2,1,0:T(8,128)} %phase_hbm.1) | copy-start | bytes 393220
  3.0 0.7 %copy-start.3 = (s32[16]{0:T(128)S(1)}, s32[16]{0:T(128)}, u32[]{:S(2)}) copy-start(s32[16]{0:T(128)} %new_slot.1) | copy-start | bytes 196

commit v2 on v1

--- a/solution.py
+++ b/solution.py
@@ -53,14 +53,15 @@
         return place
 
     around = [
-        (0, 0, 1), (1, 0, 0), (-1, 0, 0), (0, 1, 0), (0, -1, 0),
-        (1, 0, 1), (-1, 0, 1), (0, 1, 1), (0, -1, 1),
         (1, 1, 0), (-1, 1, 0), (1, -1, 0), (-1, -1, 0),
+        (0, 1, 0), (0, -1, 0), (0, 1, 1), (0, -1, 1),
+        (1, 0, 0), (-1, 0, 0), (1, 0, 1), (-1, 0, 1), (0, 0, 1),
     ]
-    partners = sorted(
-        {(a % normal, b % planes, c % 2) for a, b, c in around}
-        | {(0, k, 0) for k in range(1, planes)}
-    )
+    partners = []
+    for a, b, c in around + [(0, k, 0) for k in range(1, planes)]:
+        offset = (a % normal, b % planes, c % 2)
+        if offset not in partners:
+            partners.append(offset)
     loads = [
         pltpu.make_async_copy(source, target, load_sem.at[number])
         for number, (source, target) in enumerate(
@@ -162,6 +163,9 @@
             for x in range(width):
                 place = jnp.where(wanted == at_slot[x], places[x], place)
             info[t] = place.astype(jnp.float32)
+        return order
+
+    def send_info():
         for k in range(1, planes):
             copy = pltpu.make_async_remote_copy(
                 src_ref=info.at[lax.rem(me_x + k, planes)],
@@ -173,8 +177,9 @@
             )
             copy.start()
             info_copies.append(copy)
-        return order
-
+
+    order = plan()
+    started = []
     for step in range(STEPS):
         def potential(z, packed):
             value = 1.0 - jnp.exp(-moments[0, z])
@@ -193,29 +198,30 @@
         if step == 0:
             pl.semaphore_wait(barrier, len(partners))
         copies = start(0, step, [
-            (psi_ys.at[step], psi_yr.at[step]),
-            (psi.at[step, depth], psi.at[step, 0]),
-            (psi.at[step, 1], psi.at[step, depth + 1]),
-            (psi_xs.at[step, 0], psi_xr.at[step, 0, inner_rows]),
-            (psi_xs.at[step, 1], psi_xr.at[step, 1, inner_rows]),
-            (psi.at[step, depth], psi_zy.at[step, 0]),
-            (psi.at[step, 1], psi_zy.at[step, 1]),
-            (psi_xs.at[step, 0], psi_xyr.at[step, 0, inner_rows]),
-            (psi_xs.at[step, 1], psi_xyr.at[step, 1, inner_rows]),
             (psi_xs.at[step, 0, high], psi_xr.at[step, 0, before]),
             (psi_xs.at[step, 0, low], psi_xr.at[step, 0, after]),
             (psi_xs.at[step, 1, high], psi_xr.at[step, 1, before]),
             (psi_xs.at[step, 1, low], psi_xr.at[step, 1, after]),
+            (psi_xs.at[step, 0], psi_xr.at[step, 0, inner_rows]),
+            (psi_xs.at[step, 1], psi_xr.at[step, 1, inner_rows]),
+            (psi_xs.at[step, 0], psi_xyr.at[step, 0, inner_rows]),
+            (psi_xs.at[step, 1], psi_xyr.at[step, 1, inner_rows]),
+            (psi.at[step, depth], psi.at[step, 0]),
+            (psi.at[step, 1], psi.at[step, depth + 1]),
+            (psi.at[step, depth], psi_zy.at[step, 0]),
+            (psi.at[step, 1], psi_zy.at[step, 1]),
+            (psi_ys.at[step], psi_yr.at[step]),
         ])
         if step == 0:
-            order = plan()
+            send_info()
             loads[1].wait()
             loads[2].wait()
             lax.fori_loop(0, depth, initial, 0)
         else:
             lax.fori_loop(0, depth, prepare, 0)
         for copy in copies:
-            copy.wait()
+            copy.wait_recv()
+        started.extend(copies)
         columns = psi_yr[step]
         for side, z_at in ((0, 16), (1, 17 + depth)):
             plane_in = psi_zy[step, side]
@@ -325,19 +331,19 @@
                 pop_xs[step, side, k] = pop_rows[side, k].astype(jnp.bfloat16)
         two = pl.ds(3, 2)
         copies = start(1, step, [
-            (pop_ys.at[step], pop_yr.at[step]),
-            (pop_zs.at[step, 0], pop_zin.at[step, 0]),
-            (pop_zs.at[step, 1], pop_zin.at[step, 1]),
-            (pop_xs.at[step, 0], pop_xin.at[step, 0]),
-            (pop_xs.at[step, 1], pop_xin.at[step, 1]),
-            (pop_zs.at[step, 0, two], pop_zy.at[step, 0]),
-            (pop_zs.at[step, 1, two], pop_zy.at[step, 1]),
-            (pop_xs.at[step, 0, two], pop_xyr.at[step, 0]),
-            (pop_xs.at[step, 1, two], pop_xyr.at[step, 1]),
             (pop_xs.at[step, 0, 1], pop_zxr.at[step, 0, 0]),
             (pop_xs.at[step, 0, 2], pop_zxr.at[step, 0, 1]),
             (pop_xs.at[step, 1, 1], pop_zxr.at[step, 1, 0]),
             (pop_xs.at[step, 1, 2], pop_zxr.at[step, 1, 1]),
+            (pop_xs.at[step, 0], pop_xin.at[step, 0]),
+            (pop_xs.at[step, 1], pop_xin.at[step, 1]),
+            (pop_xs.at[step, 0, two], pop_xyr.at[step, 0]),
+            (pop_xs.at[step, 1, two], pop_xyr.at[step, 1]),
+            (pop_zs.at[step, 0], pop_zin.at[step, 0]),
+            (pop_zs.at[step, 1], pop_zin.at[step, 1]),
+            (pop_zs.at[step, 0, two], pop_zy.at[step, 0]),
+            (pop_zs.at[step, 1, two], pop_zy.at[step, 1]),
+            (pop_ys.at[step], pop_yr.at[step]),
         ])
 
         def stream(z, carry):
@@ -398,10 +404,11 @@
                 moments[7 + k, z] = cross[pair]
             return carry
 
-        copies[0].wait()
+        copies[-1].wait_recv()
         lax.fori_loop(1, depth - 1, stream, 0)
-        for copy in copies[1:]:
-            copy.wait()
+        for copy in copies[:-1]:
+            copy.wait_recv()
+        started.extend(copies)
         f32 = jnp.float32
         for k in range(5):
             pops[step, k, 0] = pop_zin[step, 0, k].astype(f32)
@@ -482,6 +489,9 @@
             copy.start()
             moves.append((g, copy))
         arrived[g, 0] = sent[g, me_x]
+
+    for copy in started:
+        copy.wait_send()
 
     for copy in info_copies:
         copy.wait()
@@ -571,7 +581,7 @@
             dma((planes,)),
         ],
         compiler_params=pltpu.CompilerParams(
-            collective_id=0, has_side_effects=True, vmem_limit_bytes=40 * 1024 * 1024
+            collective_id=0, has_side_effects=True, vmem_limit_bytes=56 * 1024 * 1024
         ),
     )(phase, velocity, stress, new_slot)
 

time: 52.9 us -> 50 us (0.945)
  local copies, waits for them, and re-layouts: 4.53 us -> 2.04 us
    unnamed x9 -> x1, local copies, waits for them, and re-layouts: 4.53 us -> 2.04 us
where the time goes in v2:
time: 50 us; the launch traced here: 49.8 us
  Pallas kernels  47.8 us (96%)
  local copies, waits for them, and re-layouts  2.04 us (4%)
    pallas_call x1, Pallas kernels, shards(): pl.pallas_call(functools.partial(kernel, (normal, planes, group_z, depth,...  47.8 us
    unnamed x1, local copies, waits for them, and re-layouts  2.04 us

profile of v2, /device:TPU:0, one launch (start us, length us, event | category | flops | bytes accessed | tf_op | source)
XLA Modules:
  0.0 49.8 jit_solution(17397278742632397498)
XLA Ops:
  0.0 47.8 %shard_map.46 = bf16[10,16,16,128]{3,2,1,0:T(8,128)(2,1)} custom-call(s32[16,16,128]{2,1,0:T(8,128)} %phase_hbm.1, f32[3,16,16,128]{3,2,1,0:T(8,128)} %velocity_hbm.1, f32[6,16,16,128]{3,2,1,0:T(8,128)} %stress_hbm.1, s32[16]{0:T(128)} %new_slot.1), custom_call_target="tpu_custom_call" | custom-call | tf_op jit(solution)/shard_map/pallas_call | solution.py:536
  47.8 2.0 %copy.6 = bf16[10,16,16,128]{3,2,1,0:T(8,128)(2,1)} copy(bf16[10,16,16,128]{3,2,1,0:T(8,128)(2,1)} %shard_map.46) | data formatting | bytes 1310720

commit v3 on v2

--- a/solution.py
+++ b/solution.py
@@ -29,8 +29,8 @@
 
 
 def kernel(
-    sizes, phase_hbm, velocity_hbm, stress_hbm, new_slot, out,
-    phase, velocity, stress, moments, speeds, psi, psi_xs, psi_xr, psi_xyr, psi_ys, psi_yr, psi_zy, psi_rows,
+    sizes, phase_hbm, velocity_hbm, stress_hbm, new_slot_hbm, out,
+    new_slot, phase, velocity, stress, moments, speeds, psi, psi_xs, psi_xr, psi_xyr, psi_ys, psi_yr, psi_zy, psi_rows,
     field_a, field_dx, field_dy, field_gx, field_gy,
     pops, pop_rows, pop_xs, pop_xin, pop_xyr, pop_zxr, pop_ys, pop_yr,
     pop_zs, pop_zin, pop_zy, side_sums, sent, arrived, info, info_in,
@@ -65,7 +65,8 @@
     loads = [
         pltpu.make_async_copy(source, target, load_sem.at[number])
         for number, (source, target) in enumerate(
-            ((phase_hbm, phase), (velocity_hbm, velocity), (stress_hbm, stress))
+            ((phase_hbm, phase), (velocity_hbm, velocity), (stress_hbm, stress),
+             (new_slot_hbm, new_slot))
         )
     ]
     for load in loads:
@@ -178,6 +179,7 @@
             copy.start()
             info_copies.append(copy)
 
+    loads[3].wait()
     order = plan()
     started = []
     for step in range(STEPS):
@@ -218,7 +220,7 @@
             loads[2].wait()
             lax.fori_loop(0, depth, initial, 0)
         else:
-            lax.fori_loop(0, depth, prepare, 0)
+            lax.fori_loop(0, depth, prepare, 0, unroll=4)
         for copy in copies:
             copy.wait_recv()
         started.extend(copies)
@@ -266,7 +268,7 @@
             )
             return carry
 
-        lax.fori_loop(0, depth + 2, differences, 0, unroll=2)
+        lax.fori_loop(0, depth + 2, differences, 0, unroll=3)
 
         def collide(z, packs):
             p = z + 1
@@ -321,7 +323,7 @@
             return up, down
 
         nothing = jnp.zeros((width, breadth), jnp.float32)
-        up, down = lax.fori_loop(0, depth, collide, (nothing, nothing))
+        up, down = lax.fori_loop(0, depth, collide, (nothing, nothing), unroll=4)
         pop_ys[step, 0] = up
         pop_ys[step, 1] = down
         for k in range(5):
@@ -405,7 +407,7 @@
             return carry
 
         copies[-1].wait_recv()
-        lax.fori_loop(1, depth - 1, stream, 0)
+        lax.fori_loop(1, depth - 1, stream, 0, unroll=7)
         for copy in copies[:-1]:
             copy.wait_recv()
         started.extend(copies)
@@ -458,11 +460,11 @@
             return carry
 
         if step < STEPS - 1:
-            lax.fori_loop(0, depth, add_sides, 0)
+            lax.fori_loop(0, depth, add_sides, 0, unroll=4)
 
     moves = []
     for g in range(groups):
-        lax.fori_loop(g * group_z, (g + 1) * group_z, add_sides, 0)
+        lax.fori_loop(g * group_z, (g + 1) * group_z, add_sides, 0, unroll=2)
         block = jnp.concatenate(
             [
                 moments[c, g * group_z : (g + 1) * group_z]
@@ -536,10 +538,10 @@
     return pl.pallas_call(
         functools.partial(kernel, (normal, planes, group_z, depth, width, breadth)),
         out_shape=jax.ShapeDtypeStruct((10, depth, width, breadth), bf16),
-        in_specs=[pl.BlockSpec(memory_space=pltpu.HBM)] * 3
-        + [pl.BlockSpec(memory_space=pltpu.SMEM)],
+        in_specs=[pl.BlockSpec(memory_space=pltpu.HBM)] * 4,
         out_specs=whole,
         scratch_shapes=[
+            pltpu.SMEM((width,), jnp.int32),
             vmem((depth,) + plane, jnp.int32),
             vmem((3, depth) + plane, f32),
             vmem((6, depth) + plane, f32),
@@ -572,7 +574,7 @@
             vmem((groups, planes, 10, 16, breadth), bf16),
             vmem((planes, 8, 128), f32),
             vmem((planes, 8, 128), f32),
-            dma((3,)),
+            dma((4,)),
             dma((2, STEPS, 13)),
             dma((2, STEPS, 13)),
             dma((groups, planes)),
@@ -581,9 +583,9 @@
             dma((planes,)),
         ],
         compiler_params=pltpu.CompilerParams(
-            collective_id=0, has_side_effects=True, vmem_limit_bytes=56 * 1024 * 1024
+            collective_id=0, has_side_effects=True, vmem_limit_bytes=40 * 1024 * 1024
         ),
-    )(phase, velocity, stress, new_slot)
+    )(*(pltpu.with_memory_space_constraint(x, pltpu.HBM) for x in (phase, velocity, stress, new_slot)))
 
 
 def solution(mesh):

time: 50 us -> 44.8 us (0.90)
  Pallas kernels: 47.8 us -> 43.9 us
  local copies, waits for them, and re-layouts: 2.04 us -> 0.84 us
    pallas_call x1, Pallas kernels: 47.8 us -> 43.9 us  [shards(): pl.pallas_call(functools.partial(kernel, (normal, planes, group_z, depth,...]
    unnamed x1, local copies, waits for them, and re-layouts: 2.04 us -> 0.84 us
where the time goes in v3:
time: 44.8 us; the launch traced here: 44.7 us
  Pallas kernels  43.9 us (98%)
  local copies, waits for them, and re-layouts  0.84 us (2%)
    pallas_call x1, Pallas kernels, shards(): pl.pallas_call(functools.partial(kernel, (normal, planes, group_z, depth,...  43.9 us

profile of v3, /device:TPU:0, one launch (start us, length us, event | category | flops | bytes accessed | tf_op | source)
XLA Modules:
  0.0 44.7 jit_solution(3854825398567843312)
XLA Ops:
  0.0 43.9 %shard_map.46 = bf16[10,16,16,128]{3,2,1,0:T(8,128)(2,1)S(1)} custom-call(s32[16,16,128]{2,1,0:T(8,128)} %phase_hbm.1, f32[3,16,16,128]{3,2,1,0:T(8,128)} %velocity_hbm.1, f32[6,16,16,128]{3,2,1,0:T(8,128)} %stress_hbm.1, s32[16]{0:T(128)} %new_slot_hbm.1), custom_call_target="tpu_custom_call" | custom-call | tf_op jit(solution)/shard_map/pallas_call | solution.py:538
  43.9 0.8 %copy.6 = bf16[10,16,16,128]{3,2,1,0:T(8,128)(2,1)} copy(bf16[10,16,16,128]{3,2,1,0:T(8,128)(2,1)S(1)} %shard_map.46) | data formatting | bytes 1310720

commit v4 on v3

--- a/solution.py
+++ b/solution.py
@@ -129,7 +129,7 @@
         return carry
 
     loads[0].wait()
-    lax.fori_loop(0, depth, start_density, 0, unroll=4)
+    lax.fori_loop(0, depth, start_density, 0, unroll=8)
 
     tile = 16
     capacity = tile // group_z
@@ -192,7 +192,7 @@
             return jnp.where(lane == z + 65, pltpu.roll(value, z + 65, 1), packed)
 
         psi_ys[step] = lax.fori_loop(
-            0, depth, potential, jnp.zeros((width, breadth), jnp.float32), unroll=4
+            0, depth, potential, jnp.zeros((width, breadth), jnp.float32), unroll=16
         )
         low, high = pl.ds(0, PAD), pl.ds(depth - PAD, PAD)
         inner_rows = pl.ds(PAD, depth)
@@ -218,7 +218,7 @@
             send_info()
             loads[1].wait()
             loads[2].wait()
-            lax.fori_loop(0, depth, initial, 0)
+            lax.fori_loop(0, depth, initial, 0, unroll=4)
         else:
             lax.fori_loop(0, depth, prepare, 0, unroll=4)
         for copy in copies:
@@ -268,7 +268,7 @@
             )
             return carry
 
-        lax.fori_loop(0, depth + 2, differences, 0, unroll=3)
+        lax.fori_loop(0, depth + 2, differences, 0, unroll=6)
 
         def collide(z, packs):
             p = z + 1
@@ -323,7 +323,7 @@
             return up, down
 
         nothing = jnp.zeros((width, breadth), jnp.float32)
-        up, down = lax.fori_loop(0, depth, collide, (nothing, nothing), unroll=4)
+        up, down = lax.fori_loop(0, depth, collide, (nothing, nothing), unroll=8)
         pop_ys[step, 0] = up
         pop_ys[step, 1] = down
         for k in range(5):
@@ -424,7 +424,7 @@
         down = jnp.where(lane == far, pltpu.roll(corner[1][1], far, 1), down)
         pop_yr[step, 0] = up
         pop_yr[step, 1] = down
-        lax.fori_loop(0, 2, lambda i, carry: stream(i * (depth - 1), carry), 0)
+        lax.fori_loop(0, 2, lambda i, carry: stream(i * (depth - 1), carry), 0, unroll=2)
 
         z_row = lax.broadcasted_iota(jnp.int32, (depth, breadth), 0)
         z_lane = lax.broadcasted_iota(jnp.int32, (depth, breadth), 1)
@@ -464,7 +464,7 @@
 
     moves = []
     for g in range(groups):
-        lax.fori_loop(g * group_z, (g + 1) * group_z, add_sides, 0, unroll=2)
+        lax.fori_loop(g * group_z, (g + 1) * group_z, add_sides, 0, unroll=4)
         block = jnp.concatenate(
             [
                 moments[c, g * group_z : (g + 1) * group_z]

time: 44.8 us -> 43.5 us (0.971)
  Pallas kernels: 43.9 us -> 42.5 us
    pallas_call x1, Pallas kernels: 43.9 us -> 42.5 us  [shards(): pl.pallas_call(functools.partial(kernel, (normal, planes, group_z, depth,...]
where the time goes in v4:
time: 43.5 us; the launch traced here: 43.4 us
  Pallas kernels  42.5 us (98%)
  local copies, waits for them, and re-layouts  0.84 us (2%)
    pallas_call x1, Pallas kernels, shards(): pl.pallas_call(functools.partial(kernel, (normal, planes, group_z, depth,...  42.5 us

profile of v4, /device:TPU:0, one launch (start us, length us, event | category | flops | bytes accessed | tf_op | source)
XLA Modules:
  0.0 43.4 jit_solution(6328129569417092101)
XLA Ops:
  0.0 42.5 %shard_map.46 = bf16[10,16,16,128]{3,2,1,0:T(8,128)(2,1)S(1)} custom-call(s32[16,16,128]{2,1,0:T(8,128)} %phase_hbm.1, f32[3,16,16,128]{3,2,1,0:T(8,128)} %velocity_hbm.1, f32[6,16,16,128]{3,2,1,0:T(8,128)} %stress_hbm.1, s32[16]{0:T(128)} %new_slot_hbm.1), custom_call_target="tpu_custom_call" | custom-call | tf_op jit(solution)/shard_map/pallas_call | solution.py:538
  42.5 0.8 %copy.6 = bf16[10,16,16,128]{3,2,1,0:T(8,128)(2,1)} copy(bf16[10,16,16,128]{3,2,1,0:T(8,128)(2,1)S(1)} %shard_map.46) | data formatting | bytes 1310720
